TPU v7x, 32 devices: a whole 2x2x4 slice. The times are simulated.
32 devices in a mesh: box: 32 (over z, y, x, core), exc: 1.
Axes of the slice: x: 2, y: 2, z: 4, core: 2. Of those that a mesh axis runs over, the one named last changes fastest.
Arguments:
- incident: bfloat16 [2, 2, 128, 512], P(None, 'exc', 'box'), may hold values from -7 to 7
- contrast: int32 [128, 512], P('box'), may hold values from 1 to 16
- box_pos: int32 [128], replicated, may hold values from 0 to 3, as said below
- directions: float32 [3, 512], P(None, 'box'), may hold values from -1 to 1, as said below
- enc_table: bfloat16 [2, 512, 512], replicated, may hold values from -0.25 to 0.25
- dec_table: bfloat16 [2, 512, 512], replicated, may hold values from -0.25 to 0.25
Outputs:
- scattered_one: bfloat16 [2, 2, 128, 512], P(None, 'exc', 'box')
- scattered_two: bfloat16 [2, 2, 128, 512], P(None, 'exc', 'box')
- series_ratio: float32 [128], P('box')
Inputs may be any that keep to these rules, and one draw needn't show every extreme that they name: `box_pos`: entries 4 m to 4 m + 3 hold each number from 0 to 3 once. `directions`: each column is a unit vector.
All inputs are finite; a program needn't handle non-finite values.
Results may differ from a plain program's by a relative error of at most 0.0053.
Values may be sent and summed in bfloat16 or wider, within the bound.
A program may use at most 128 MiB of HBM per device.

v0:
```python
import functools

import jax
import jax.numpy as jnp
import ml_dtypes
import numpy as np
from jax import lax
from jax.experimental import pallas as pl
from jax.experimental.pallas import tpu as pltpu
from jax.sharding import PartitionSpec as P

BSIDE = 8
CY = 2
CZ = 2
BOX_DEV = CY * CZ
ROWS = 4 * BOX_DEV
LANES = 128
TERMS = 16
MESH = pl.DeviceIdType.MESH

wave_number = 0.8
near_scale = 0.1
self_value = 1.0
far_scale = 0.25
chi_step = 0.0625
epsilon = 1e-06

F32 = jnp.float32
BF16 = jnp.bfloat16


def harmonics(x, y, z):
    s3, s6, s10, s15 = 3.0**0.5, 6.0**0.5, 10.0**0.5, 15.0**0.5
    xx, yy, zz = x * x, y * y, z * z
    return [
        (0, x * 0.0 + 1.0),
        (1, x),
        (1, y),
        (1, z),
        (2, s3 * x * y),
        (2, s3 * y * z),
        (2, s3 * x * z),
        (2, 0.5 * (2.0 * zz - xx - yy)),
        (2, 0.5 * s3 * (xx - yy)),
        (3, 0.5 * z * (2.0 * zz - 3.0 * xx - 3.0 * yy)),
        (3, 0.25 * s6 * x * (4.0 * zz - xx - yy)),
        (3, 0.25 * s6 * y * (4.0 * zz - xx - yy)),
        (3, 0.5 * s15 * z * (xx - yy)),
        (3, s15 * x * y * z),
        (3, 0.25 * s10 * x * (xx - 3.0 * yy)),
        (3, 0.25 * s10 * y * (3.0 * xx - yy)),
    ]


def near_planes():
    slot = np.arange(BOX_DEV * BSIDE * BSIDE)
    box, inner = slot // (BSIDE * BSIDE), slot % (BSIDE * BSIDE)
    row = box // CZ * BSIDE + inner // BSIDE
    col = box % CZ * BSIDE + inner % BSIDE
    gap = np.arange(2 * BSIDE)[:, None, None]
    square = gap**2 + (row[:, None] - row[None]) ** 2 + (col[:, None] - col[None]) ** 2
    radius = np.sqrt(np.maximum(square, 1).astype(np.float64))
    wave = near_scale * np.exp(1j * wave_number * radius) / radius
    wave = np.where(square == 0, self_value, wave)
    return np.concatenate([wave.real, wave.imag], axis=2).astype(ml_dtypes.bfloat16)


def far_terms(slabs):
    lane = np.arange(slabs * 8)
    slab = lane // 16 * 2 + lane % 2
    box = lane // 4 % 4
    part = lane // 2 % 2
    coords = np.stack([slab, box // CZ, box % CZ]).astype(np.float64)
    gap = coords[:, None, :] - coords[:, :, None]
    nearby = np.abs(gap).max(0) < 1.5
    radius = np.sqrt(np.maximum((gap**2).sum(0), 1.0))
    kappa = wave_number * BSIDE
    arg = kappa * radius
    before, now = np.exp(1j * arg) / arg, -1j * np.exp(1j * arg) / arg
    radial = []
    for order in range(4):
        value = (2 * order + 1) * 1j**order * now * far_scale * kappa / 16.0
        radial.append(np.where(nearby, 0.0, value))
        before, now = now, (2 * order + 1) * now / arg - before
    source, target = part[:, None], part[None, :]
    out = np.empty((TERMS, slabs * 8, slabs * 8), ml_dtypes.bfloat16)
    for term, (order, value) in enumerate(harmonics(*(gap / radius))):
        h = radial[order] * value
        cross = np.where(source == 0, h.imag, -h.imag)
        out[term] = np.where(source == target, h.real, cross).astype(ml_dtypes.bfloat16)
    return out


def nt(left, right):
    return lax.dot_general(left, right, (((1,), (1,)), ((), ())), preferred_element_type=F32)


def nn(left, right):
    return lax.dot_general(left, right, (((1,), (0,)), ((), ())), preferred_element_type=F32)


def times_i(x):
    rows = x.shape[0]
    row = lax.broadcasted_iota(jnp.int32, x.shape, 0)
    return jnp.where(row // 2 % 2 == 0, -pltpu.roll(x, rows - 2, 0), pltpu.roll(x, 2, 0))


def kernel(
    n, kdev, kpad, single, inc_ref, con_ref, pos_ref, dir_ref, enc_hbm, dec_hbm, near_hbm, far_hbm,
    one_ref, two_ref, rat_ref,
    enc_v, dec_v, near_v, far_v, own_x, nbr_x, snd, rcv, side_s, side_r, flat,
    load_sem, send_sem, recv_sem, side_ss, side_rs,
):
    me = lax.axis_index("box")
    barrier = pltpu.get_barrier_semaphore()

    def greet(j, carry):
        pl.semaphore_signal(barrier, inc=1, device_id={"box": lax.rem(me + j, n)}, device_id_type=MESH)
        return carry

    lax.fori_loop(1, n, greet, 0)
    loads = [
        pltpu.make_async_copy(hbm, vmem, load_sem.at[i])
        for i, (hbm, vmem) in enumerate(
            ((enc_hbm, enc_v), (near_hbm, near_v), (far_hbm, far_v), (dec_hbm, dec_v))
        )
    ]
    for load in loads:
        load.start()

    row = lax.broadcasted_iota(jnp.int32, (ROWS, ROWS), 0)
    col = lax.broadcasted_iota(jnp.int32, (ROWS, ROWS), 1)

    def spread(index):
        out = jnp.zeros((ROWS, ROWS), jnp.int32)
        for b in range(BOX_DEV):
            out = jnp.where(index % 4 == b, pos_ref[me * BOX_DEV + b], out)
        return out

    to_grid = jnp.where((row % 4 == col // 4) & (spread(col) == row // 4), 1.0, 0.0).astype(BF16)
    from_grid = jnp.where((col % 4 == row // 4) & (spread(row) == col // 4), 1.0, 0.0).astype(BF16)
    pieces = [inc_ref[a, e].astype(F32) for a in range(2) for e in range(2)]
    field = nn(to_grid, jnp.concatenate(pieces, axis=0).astype(BF16))
    step = con_ref[...].astype(F32) * chi_step
    own_pick = jnp.where((spread(col) == row // 4) & (col < 4), 1.0, 0.0).astype(BF16)
    chi = nn(own_pick, jnp.concatenate([step, jnp.zeros((12, step.shape[1]), F32)], axis=0).astype(BF16))

    drow = lax.broadcasted_iota(jnp.int32, (kpad, kdev), 0)
    dcol = lax.broadcasted_iota(jnp.int32, (kpad, kdev), 1)
    column = [
        jnp.sum(jnp.where(drow == dcol, dir_ref[c : c + 1, :], 0.0), axis=1, keepdims=True)
        for c in range(3)
    ]
    weights = [jnp.concatenate([y, y], axis=0) for _, y in harmonics(*column)]

    lane = lax.broadcasted_iota(jnp.int32, (kpad, LANES), 1)
    even = lane % 2 == 0
    own_x[...] = jnp.zeros_like(own_x)
    nbr_x[...] = jnp.zeros_like(nbr_x)
    if kdev != kpad:
        snd[...] = jnp.zeros_like(snd)
    plane = BSIDE * BSIDE

    def near_sum(ext, low, high):
        total = jnp.zeros((32, 2 * near_v.shape[1]), F32)
        for d in range(low, high):
            if d == 0:
                total += nn(ext[64:96, :].astype(BF16), near_v[0])
            else:
                both = jnp.concatenate([ext[64 + 4 * d : 96 + 4 * d, :], ext[64 - 4 * d : 96 - 4 * d, :]], axis=0)
                got = nn(both.astype(BF16), near_v[d])
                total += got[:32] + got[32:]
        return total

    def exchange(phase):
        def send(j, carry):
            there = lax.rem(me + j, n)
            pltpu.make_async_remote_copy(
                src_ref=snd.at[phase, there],
                dst_ref=rcv.at[phase, me],
                send_sem=send_sem.at[phase],
                recv_sem=recv_sem.at[phase],
                device_id={"box": there},
                device_id_type=MESH,
            ).start()
            return carry

        lax.fori_loop(1, n, send, 0)
        rcv[phase, pl.ds(me, 1)] = snd[phase, pl.ds(me, 1)]

    def arrived(phase):
        part = rcv.at[phase, pl.ds(0, n - 1)]
        pltpu.make_async_copy(part, part, recv_sem.at[phase]).wait()

    sums = []
    for turn in range(2):
        source = (chi * field).astype(BF16).astype(F32)
        planes = jnp.concatenate(
            [
                jnp.concatenate(
                    [source[4 * g : 4 * g + 4, x * plane : (x + 1) * plane] for g in range(BOX_DEV)], axis=1
                )
                for x in range(BSIDE)
            ],
            axis=0,
        )
        own_x[64:96, :] = planes
        side_s[turn] = planes.astype(BF16)
        if turn == 0:
            pl.semaphore_wait(barrier, n - 1)
        sides = []
        for s, away in enumerate((1, n - 1)):
            sides.append(
                pltpu.make_async_remote_copy(
                    src_ref=side_s.at[turn],
                    dst_ref=side_r.at[turn, s],
                    send_sem=side_ss.at[turn, s],
                    recv_sem=side_rs.at[turn, s],
                    device_id={"box": lax.rem(me + away, n)},
                    device_id_type=MESH,
                )
            )
            sides[-1].start()
        if turn == 0:
            loads[0].wait()
        first = jnp.concatenate([source, jnp.zeros((LANES - ROWS, source.shape[1]), F32)], axis=0)
        second = jnp.concatenate([times_i(source), jnp.zeros((LANES - ROWS, source.shape[1]), F32)], axis=0)
        encoded = nt(enc_v[0], first.astype(BF16)) + nt(enc_v[1], second.astype(BF16))
        if kdev == kpad:
            snd[2 * turn] = encoded.reshape(n, kdev, LANES).astype(BF16)
        else:
            for d in range(n):
                snd[2 * turn, d, :kdev, :] = encoded[d * kdev : (d + 1) * kdev, :].astype(BF16)
        exchange(2 * turn)

        if turn == 0:
            loads[1].wait()
        near = near_sum(own_x, 0, BSIDE)

        arrived(2 * turn)
        columns = [[], []]
        for group in range(n // 16):
            sum0, sum1 = (jnp.zeros((kpad, LANES), F32) for _ in range(2))
            for pair in range(8):
                a = rcv[2 * turn, group * 16 + pair * 2].astype(F32)
                b = rcv[2 * turn, group * 16 + pair * 2 + 1].astype(F32)
                exc0 = jnp.where(even, a, pltpu.roll(b, 1, 1))
                exc1 = jnp.where(even, pltpu.roll(a, LANES - 1, 1), b)
                if pair:
                    exc0, exc1 = pltpu.roll(exc0, 16 * pair, 1), pltpu.roll(exc1, 16 * pair, 1)
                sum0, sum1 = sum0 + exc0, sum1 + exc1
            columns[0].append(sum0)
            columns[1].append(sum1)
        waves = jnp.concatenate([jnp.concatenate(c, axis=1) for c in columns], axis=0).astype(BF16)
        if turn == 0:
            loads[2].wait()
        moved = jnp.zeros((2 * kpad, n * 8), F32)
        for term in range(TERMS):
            moved += weights[term] * nn(waves, far_v[term])
        for group in range(n // 16):
            out0 = moved[:kpad, group * LANES : (group + 1) * LANES]
            out1 = moved[kpad:, group * LANES : (group + 1) * LANES]
            for pair in range(8):
                a, b = out0, out1
                if pair:
                    a, b = pltpu.roll(a, LANES - 16 * pair, 1), pltpu.roll(b, LANES - 16 * pair, 1)
                slab = group * 16 + pair * 2
                snd[2 * turn + 1, slab] = jnp.where(even, a, pltpu.roll(b, 1, 1)).astype(BF16)
                snd[2 * turn + 1, slab + 1] = jnp.where(even, pltpu.roll(a, LANES - 1, 1), b).astype(BF16)
        exchange(2 * turn + 1)

        for side in sides:
            side.wait()
        nbr_x[32:64, :] = jnp.where(me > 0, side_r[turn, 0].astype(F32), 0.0)
        nbr_x[96:128, :] = jnp.where(me < n - 1, side_r[turn, 1].astype(F32), 0.0)
        near = near + near_sum(nbr_x, 1, 2 * BSIDE)
        half = near.shape[1] // 2
        near = near[:, :half] + times_i(near[:, half:])
        near = jnp.concatenate(
            [
                jnp.concatenate(
                    [near[4 * x : 4 * x + 4, g * plane : (g + 1) * plane] for x in range(BSIDE)], axis=1
                )
                for g in range(BOX_DEV)
            ],
            axis=0,
        )

        arrived(2 * turn + 1)
        if kdev == kpad:
            back = rcv[2 * turn + 1].astype(F32).reshape(n * kdev, LANES)
        else:
            for d in range(n):
                flat[d * kdev : (d + 1) * kdev, :] = rcv[2 * turn + 1, d].astype(F32)[:kdev, :]
            back = flat[...]
        back = jnp.transpose(back)[:ROWS]
        if turn == 0:
            loads[3].wait()
        far = nt(back.astype(BF16), dec_v[0]) + nt(times_i(back).astype(BF16), dec_v[1])
        rounded = (near + far).astype(BF16)
        result = nn(from_grid, rounded)
        out_ref = one_ref if turn == 0 else two_ref
        for a in range(2):
            for e in range(2):
                start = (2 * a + e) * BOX_DEV
                out_ref[a, e] = result[start : start + BOX_DEV].astype(BF16)
        field = rounded.astype(F32)
        square = jnp.sum(result * result, axis=1, keepdims=True)
        sums.append(square[:4] + square[4:8] + square[8:12] + square[12:])

    for phase in range(4):
        part = snd.at[phase, pl.ds(0, n - 1)]
        pltpu.make_async_copy(part, part, send_sem.at[phase]).wait()

    count = 4 * inc_ref.shape[3]
    if single:
        values = [jnp.sqrt(sums[1] / count / (sums[0] / count + epsilon))]
    else:
        values = sums
    brow = lax.broadcasted_iota(jnp.int32, (BOX_DEV, 1), 0)
    for i, value in enumerate(values):
        for b in range(BOX_DEV):
            rat_ref[i * BOX_DEV + b] = jnp.sum(jnp.where(brow == b, value, 0.0))


def shards(incident, contrast, box_pos, directions, enc_table, dec_table):
    n = lax.axis_size("box")
    exc_axis = lax.axis_size("exc")
    single = exc_axis == 1
    kdev = directions.shape[1]
    kpad = max(kdev, 16)
    near_np, far_np = near_planes(), far_terms(n)
    vmem = pl.BlockSpec(memory_space=pltpu.VMEM)
    smem = pl.BlockSpec(memory_space=pltpu.SMEM)
    anyspace = pl.BlockSpec(memory_space=pl.ANY)
    width = near_np.shape[1]
    one, two, ratio = pl.pallas_call(
        functools.partial(kernel, n, kdev, kpad, single),
        out_shape=(
            jax.ShapeDtypeStruct(incident.shape, BF16),
            jax.ShapeDtypeStruct(incident.shape, BF16),
            jax.ShapeDtypeStruct((BOX_DEV if single else 2 * BOX_DEV,), F32),
        ),
        in_specs=[vmem, vmem, smem, vmem, anyspace, anyspace, anyspace, anyspace],
        out_specs=(vmem, vmem, smem),
        scratch_shapes=[
            pltpu.VMEM(enc_table.shape, BF16),
            pltpu.VMEM(dec_table.shape, BF16),
            pltpu.VMEM(near_np.shape, BF16),
            pltpu.VMEM(far_np.shape, BF16),
            pltpu.VMEM((160, width), F32),
            pltpu.VMEM((160, width), F32),
            pltpu.VMEM((4, n, kpad, LANES), BF16),
            pltpu.VMEM((4, n, kpad, LANES), BF16),
            pltpu.VMEM((2, 32, width), BF16),
            pltpu.VMEM((2, 2, 32, width), BF16),
            pltpu.VMEM((n * kdev, LANES), F32),
            pltpu.SemaphoreType.DMA((4,)),
            pltpu.SemaphoreType.DMA((4,)),
            pltpu.SemaphoreType.DMA((4,)),
            pltpu.SemaphoreType.DMA((2, 2)),
            pltpu.SemaphoreType.DMA((2, 2)),
        ],
        compiler_params=pltpu.CompilerParams(
            collective_id=0, has_side_effects=True, vmem_limit_bytes=56 * 1024 * 1024
        ),
    )(
        incident, contrast, box_pos, directions, enc_table, dec_table, jnp.asarray(near_np), jnp.asarray(far_np)
    )
    if not single:
        sums = lax.psum(ratio.reshape(2, BOX_DEV), "exc")
        count = 4 * incident.shape[3] * exc_axis
        ratio = jnp.sqrt(sums[1] / count / (sums[0] / count + epsilon))
    return one, two, ratio


def solution(mesh):
    placed = (P(None, "exc", "box", None), P("box", None), P(), P(None, "box"), P(), P())
    return jax.shard_map(
        shards,
        mesh=mesh,
        in_specs=placed,
        out_specs=(P(None, "exc", "box", None), P(None, "exc", "box", None), P("box")),
        check_vma=False,
    )
```

profile of v0, /device:TPU:0, one launch (start us, length us, event | category | flops | bytes accessed | tf_op | source)
XLA Modules:
  0.0 38.9 jit_solution(2114769188237115187)
XLA Ops:
  0.6 34.4 %shard_map.103 = (bf16[2,2,4,512]{3,2,1,0:T(4,128)(2,1)}, bf16[2,2,4,512]{3,2,1,0:T(4,128)(2,1)}, f32[4]{0:T(128)}) custom-call(bf16[2,2,4,512]{3,2,1,0:T(4,128)(2,1)} %inc_ref.1, s32[4,512]{1,0:T(4,128)} %con_ref.1, s32[128]{0:T(128)} %pos_ref.1, f32[3,16]{1,0:T(4,128)} %dir_ref.1, bf16[2,512,512]{2,1,0:T(8,128)(2,1)} %enc_hbm.1, ...), custom_call_target="tpu_custom_call" | custom-call | tf_op jit(solution)/shard_map/pallas_call | solution.py:337
  35.0 1.3 %copy.14 = bf16[2,2,4,512]{3,2,1,0:T(4,128)(2,1)} copy(bf16[2,2,4,512]{3,2,1,0:T(4,128)(2,1)} %get-tuple-element.6) | data formatting | bytes 32768
  36.4 1.3 %copy.15 = bf16[2,2,4,512]{3,2,1,0:T(4,128)(2,1)} copy(bf16[2,2,4,512]{3,2,1,0:T(4,128)(2,1)} %get-tuple-element.7) | data formatting | bytes 32768
  37.7 1.2 %copy.16 = f32[4]{0:T(128)} copy(f32[4]{0:T(128)} %get-tuple-element.8) | data formatting | bytes 32
where the time goes:
time: 39.3 us; the launch traced here: 38.9 us
  Pallas kernels  34.4 us (88%)
  local copies, waits for them, and re-layouts  3.84 us (10%)
  between operations  0.64 us (2%)
    pallas_call x1, Pallas kernels, shards(): pl.pallas_call(functools.partial(kernel, n, kdev, kpad, single), out_shap...  34.4 us
    unnamed x3, local copies, waits for them, and re-layouts  3.84 us

commit v1 on v0

--- a/solution.py
+++ b/solution.py
@@ -118,7 +118,7 @@
         pl.semaphore_signal(barrier, inc=1, device_id={"box": lax.rem(me + j, n)}, device_id_type=MESH)
         return carry
 
-    lax.fori_loop(1, n, greet, 0)
+    lax.fori_loop(1, n, greet, 0, unroll=n <= 32)
     loads = [
         pltpu.make_async_copy(hbm, vmem, load_sem.at[i])
         for i, (hbm, vmem) in enumerate(
@@ -185,7 +185,7 @@
             ).start()
             return carry
 
-        lax.fori_loop(1, n, send, 0)
+        lax.fori_loop(1, n, send, 0, unroll=n <= 32)
         rcv[phase, pl.ds(me, 1)] = snd[phase, pl.ds(me, 1)]
 
     def arrived(phase):
@@ -321,6 +321,13 @@
     for i, value in enumerate(values):
         for b in range(BOX_DEV):
             rat_ref[i * BOX_DEV + b] = jnp.sum(jnp.where(brow == b, value, 0.0))
+
+
+def finish(one_in, two_in, rat_in, one_ref, two_ref, rat_ref):
+    one_ref[...] = one_in[...]
+    two_ref[...] = two_in[...]
+    for b in range(BOX_DEV):
+        rat_ref[b] = rat_in[b]
 
 
 def shards(incident, contrast, box_pos, directions, enc_table, dec_table):
@@ -371,7 +378,12 @@
         sums = lax.psum(ratio.reshape(2, BOX_DEV), "exc")
         count = 4 * incident.shape[3] * exc_axis
         ratio = jnp.sqrt(sums[1] / count / (sums[0] / count + epsilon))
-    return one, two, ratio
+    return pl.pallas_call(
+        finish,
+        out_shape=[jax.ShapeDtypeStruct(x.shape, x.dtype) for x in (one, two, ratio)],
+        in_specs=[vmem, vmem, smem],
+        out_specs=[vmem, vmem, smem],
+    )(one, two, ratio)
 
 
 def solution(mesh):

time: 39.3 us -> 36.6 us (0.931)
  local copies, waits for them, and re-layouts: 3.84 us -> 0 us
  Pallas kernels: 34.4 us -> 35.7 us
    unnamed x3 -> x0, local copies, waits for them, and re-layouts: 3.84 us -> none
    pallas_call x0 -> x1, Pallas kernels: none -> 1.42 us  [shards(): pl.pallas_call(finish, out_shape=[jax.ShapeDtypeStruct(x.shape, x.dtype)...]
where the time goes in v1:
time: 36.6 us; the launch traced here: 36.3 us
  Pallas kernels  35.7 us (98%)
  between operations  0.64 us (2%)
    pallas_call x1, Pallas kernels, shards(): pl.pallas_call(functools.partial(kernel, n, kdev, kpad, single), out_shap...  34.3 us
    pallas_call x1, Pallas kernels, shards(): pl.pallas_call(finish, out_shape=[jax.ShapeDtypeStruct(x.shape, x.dtype)...  1.42 us

profile of v1, /device:TPU:0, one launch (start us, length us, event | category | flops | bytes accessed | tf_op | source)
XLA Modules:
  0.0 36.3 jit_solution(9175439017085514616)
XLA Ops:
  0.6 34.3 %shard_map.103 = (bf16[2,2,4,512]{3,2,1,0:T(4,128)(2,1)}, bf16[2,2,4,512]{3,2,1,0:T(4,128)(2,1)}, f32[4]{0:T(128)}) custom-call(bf16[2,2,4,512]{3,2,1,0:T(4,128)(2,1)} %inc_ref.1, s32[4,512]{1,0:T(4,128)} %con_ref.1, s32[128]{0:T(128)} %pos_ref.1, f32[3,16]{1,0:T(4,128)} %dir_ref.1, bf16[2,512,512]{2,1,0:T(8,128)(2,1)} %enc_hbm.1, ...), custom_call_target="tpu_custom_call" | custom-call | tf_op jit(solution)/shard_map/pallas_call | solution.py:344
  34.9 1.4 %shard_map.104 = (bf16[2,2,4,512]{3,2,1,0:T(4,128)(2,1)}, bf16[2,2,4,512]{3,2,1,0:T(4,128)(2,1)}, f32[4]{0:T(128)}) custom-call(bf16[2,2,4,512]{3,2,1,0:T(4,128)(2,1)} %get-tuple-element.6.one_in, bf16[2,2,4,512]{3,2,1,0:T(4,128)(2,1)} %get-tuple-element.7.two_in, f32[4]{0:T(128)} %get-tuple-element.8.rat_in), custom_call_target="tpu_custom_call" | custom-call | tf_op jit(solution)/shard_map/pallas_call | solution.py:381

commit v2 on v1

--- a/solution.py
+++ b/solution.py
@@ -160,6 +160,29 @@
     if kdev != kpad:
         snd[...] = jnp.zeros_like(snd)
     plane = BSIDE * BSIDE
+
+    direction = lax.broadcasted_iota(jnp.int32, (kpad, LANES), 0)
+    mine = direction % 8 == lane // ROWS
+
+    def pack(x):
+        if kdev != kpad:
+            return x.astype(BF16)
+        x = jnp.where(mine, x, 0.0)
+        return jnp.concatenate([jnp.sum(x[h : h + 8], axis=0, keepdims=True) for h in range(0, kpad, 8)], axis=0)
+
+    def unpack(x):
+        if kdev != kpad:
+            return jnp.where(lane < ROWS, x, 0.0)
+        rows = [jnp.broadcast_to(x[h : h + 1], (8, LANES)) for h in range(kpad // 8)]
+        return jnp.where(mine, jnp.concatenate(rows, axis=0), 0.0)
+
+    def stagger(x, shift):
+        if kdev != kpad:
+            return x
+        out = x
+        for j in range(1, 8):
+            out = jnp.where(direction % 8 == j, pltpu.roll(x, shift * j % LANES, 1), out)
+        return out
 
     def near_sum(ext, low, high):
         total = jnp.zeros((32, 2 * near_v.shape[1]), F32)
@@ -223,11 +246,12 @@
             sides[-1].start()
         if turn == 0:
             loads[0].wait()
-        first = jnp.concatenate([source, jnp.zeros((LANES - ROWS, source.shape[1]), F32)], axis=0)
-        second = jnp.concatenate([times_i(source), jnp.zeros((LANES - ROWS, source.shape[1]), F32)], axis=0)
+        first = jnp.concatenate([source] * (LANES // ROWS), axis=0)
+        second = jnp.concatenate([times_i(source)] * (LANES // ROWS), axis=0)
         encoded = nt(enc_v[0], first.astype(BF16)) + nt(enc_v[1], second.astype(BF16))
         if kdev == kpad:
-            snd[2 * turn] = encoded.reshape(n, kdev, LANES).astype(BF16)
+            for d in range(n):
+                snd[2 * turn, d] = pack(encoded[d * kdev : (d + 1) * kdev, :])
         else:
             for d in range(n):
                 snd[2 * turn, d, :kdev, :] = encoded[d * kdev : (d + 1) * kdev, :].astype(BF16)
@@ -242,15 +266,15 @@
         for group in range(n // 16):
             sum0, sum1 = (jnp.zeros((kpad, LANES), F32) for _ in range(2))
             for pair in range(8):
-                a = rcv[2 * turn, group * 16 + pair * 2].astype(F32)
-                b = rcv[2 * turn, group * 16 + pair * 2 + 1].astype(F32)
+                a = unpack(rcv[2 * turn, group * 16 + pair * 2].astype(F32))
+                b = unpack(rcv[2 * turn, group * 16 + pair * 2 + 1].astype(F32))
                 exc0 = jnp.where(even, a, pltpu.roll(b, 1, 1))
                 exc1 = jnp.where(even, pltpu.roll(a, LANES - 1, 1), b)
                 if pair:
                     exc0, exc1 = pltpu.roll(exc0, 16 * pair, 1), pltpu.roll(exc1, 16 * pair, 1)
                 sum0, sum1 = sum0 + exc0, sum1 + exc1
-            columns[0].append(sum0)
-            columns[1].append(sum1)
+            columns[0].append(stagger(sum0, LANES - ROWS))
+            columns[1].append(stagger(sum1, LANES - ROWS))
         waves = jnp.concatenate([jnp.concatenate(c, axis=1) for c in columns], axis=0).astype(BF16)
         if turn == 0:
             loads[2].wait()
@@ -258,15 +282,15 @@
         for term in range(TERMS):
             moved += weights[term] * nn(waves, far_v[term])
         for group in range(n // 16):
-            out0 = moved[:kpad, group * LANES : (group + 1) * LANES]
-            out1 = moved[kpad:, group * LANES : (group + 1) * LANES]
+            out0 = stagger(moved[:kpad, group * LANES : (group + 1) * LANES], ROWS)
+            out1 = stagger(moved[kpad:, group * LANES : (group + 1) * LANES], ROWS)
             for pair in range(8):
                 a, b = out0, out1
                 if pair:
                     a, b = pltpu.roll(a, LANES - 16 * pair, 1), pltpu.roll(b, LANES - 16 * pair, 1)
                 slab = group * 16 + pair * 2
-                snd[2 * turn + 1, slab] = jnp.where(even, a, pltpu.roll(b, 1, 1)).astype(BF16)
-                snd[2 * turn + 1, slab + 1] = jnp.where(even, pltpu.roll(a, LANES - 1, 1), b).astype(BF16)
+                snd[2 * turn + 1, slab] = pack(jnp.where(even, a, pltpu.roll(b, 1, 1)))
+                snd[2 * turn + 1, slab + 1] = pack(jnp.where(even, pltpu.roll(a, LANES - 1, 1), b))
         exchange(2 * turn + 1)
 
         for side in sides:
@@ -288,12 +312,16 @@
 
         arrived(2 * turn + 1)
         if kdev == kpad:
-            back = rcv[2 * turn + 1].astype(F32).reshape(n * kdev, LANES)
+            back = jnp.concatenate([unpack(rcv[2 * turn + 1, d]) for d in range(n)], axis=0)
         else:
             for d in range(n):
                 flat[d * kdev : (d + 1) * kdev, :] = rcv[2 * turn + 1, d].astype(F32)[:kdev, :]
             back = flat[...]
-        back = jnp.transpose(back)[:ROWS]
+        back = jnp.transpose(back)
+        if kdev == kpad:
+            back = sum(back[c * ROWS : (c + 1) * ROWS] for c in range(LANES // ROWS))
+        else:
+            back = back[:ROWS]
         if turn == 0:
             loads[3].wait()
         far = nt(back.astype(BF16), dec_v[0]) + nt(times_i(back).astype(BF16), dec_v[1])
@@ -341,6 +369,7 @@
     smem = pl.BlockSpec(memory_space=pltpu.SMEM)
     anyspace = pl.BlockSpec(memory_space=pl.ANY)
     width = near_np.shape[1]
+    message = ((4, n, kpad // 8, LANES), F32) if kdev == kpad else ((4, n, kpad, LANES), BF16)
     one, two, ratio = pl.pallas_call(
         functools.partial(kernel, n, kdev, kpad, single),
         out_shape=(
@@ -357,8 +386,8 @@
             pltpu.VMEM(far_np.shape, BF16),
             pltpu.VMEM((160, width), F32),
             pltpu.VMEM((160, width), F32),
-            pltpu.VMEM((4, n, kpad, LANES), BF16),
-            pltpu.VMEM((4, n, kpad, LANES), BF16),
+            pltpu.VMEM(*message),
+            pltpu.VMEM(*message),
             pltpu.VMEM((2, 32, width), BF16),
             pltpu.VMEM((2, 2, 32, width), BF16),
             pltpu.VMEM((n * kdev, LANES), F32),

time: 36.6 us -> 34.3 us (0.937)
  Pallas kernels: 35.7 us -> 33.3 us
    pallas_call x1, Pallas kernels: 34.3 us -> 31.9 us  [shards(): pl.pallas_call(functools.partial(kernel, n, kdev, kpad, single), out_shap...]
where the time goes in v2:
time: 34.3 us; the launch traced here: 34 us
  Pallas kernels  33.3 us (97%)
  between operations  0.64 us (2%)
    pallas_call x1, Pallas kernels, shards(): pl.pallas_call(functools.partial(kernel, n, kdev, kpad, single), out_shap...  31.9 us
    pallas_call x1, Pallas kernels, shards(): pl.pallas_call(finish, out_shape=[jax.ShapeDtypeStruct(x.shape, x.dtype)...  1.42 us

profile of v2, /device:TPU:0, one launch (start us, length us, event | category | flops | bytes accessed | tf_op | source)
XLA Modules:
  0.0 34.0 jit_solution(18144852439054950285)
XLA Ops:
  0.6 31.9 %shard_map.103 = (bf16[2,2,4,512]{3,2,1,0:T(4,128)(2,1)}, bf16[2,2,4,512]{3,2,1,0:T(4,128)(2,1)}, f32[4]{0:T(128)}) custom-call(bf16[2,2,4,512]{3,2,1,0:T(4,128)(2,1)} %inc_ref.1, s32[4,512]{1,0:T(4,128)} %con_ref.1, s32[128]{0:T(128)} %pos_ref.1, f32[3,16]{1,0:T(4,128)} %dir_ref.1, bf16[2,512,512]{2,1,0:T(8,128)(2,1)} %enc_hbm.1, ...), custom_call_target="tpu_custom_call" | custom-call | tf_op jit(solution)/shard_map/pallas_call | solution.py:373
  32.6 1.4 %shard_map.104 = (bf16[2,2,4,512]{3,2,1,0:T(4,128)(2,1)}, bf16[2,2,4,512]{3,2,1,0:T(4,128)(2,1)}, f32[4]{0:T(128)}) custom-call(bf16[2,2,4,512]{3,2,1,0:T(4,128)(2,1)} %get-tuple-element.6.one_in, bf16[2,2,4,512]{3,2,1,0:T(4,128)(2,1)} %get-tuple-element.7.two_in, f32[4]{0:T(128)} %get-tuple-element.8.rat_in), custom_call_target="tpu_custom_call" | custom-call | tf_op jit(solution)/shard_map/pallas_call | solution.py:410
